TPU v7x, 1024 devices: a whole 4x8x16 slice. The times are simulated.
1024 devices in a mesh: energy: 64 (over x, y, core), domain: 16 (over z).
Axes of the slice: x: 4, y: 8, z: 16, core: 2. Of those that a mesh axis runs over, the one named last changes fastest.
Arguments:
- hamilton: float32 [16, 256, 256], P('domain'), may hold values from -0.04 to 1.56, as said below
- coupling: float32 [16, 256, 256], P('domain'), may hold values from -0.6 to 0
- left_contact: float32 [64, 256, 256], P('energy'), may hold values from -0.5 to 3, as said below
- right_contact: float32 [64, 256, 256], P('energy'), may hold values from -0.3 to 1.8, as said below
- shifts: float32 [64], P('energy'), may hold values from 0.001 to 0.016
- coulomb: float32 [16, 256, 256], P('domain', 'energy'), may hold values from 0.08 to 0.32
Outputs:
- self_energy: bfloat16 [64, 16, 256, 256], P('energy', 'domain')
Inputs may be any that keep to these rules, and one draw needn't show every extreme that they name: `hamilton`: each block is symmetric. `left_contact`: each block is symmetric. `right_contact`: each block is symmetric.
All inputs are finite; a program needn't handle non-finite values.
Results may differ from a plain program's by a relative error of at most 0.0035.
Values may be sent and summed in bfloat16 or wider, within the bound.
A program may use at most 64 MiB of HBM per device.

v0:
```python
import math

import jax
import jax.numpy as jnp
from jax import lax
from jax.sharding import PartitionSpec as P


def passed_along(array, axis, by):
    length = lax.axis_size(axis)
    pairs = [(i, i + by) for i in range(length) if 0 <= i + by < length]
    return lax.ppermute(array, axis, pairs)


def matmul_hi(left, right):
    return jnp.matmul(left, right, precision=lax.Precision.HIGHEST)


def flip(matrix):
    return jnp.swapaxes(matrix, -1, -2)


def spd_solve(matrix, target):
    factor = jnp.linalg.cholesky(matrix)
    return jax.scipy.linalg.cho_solve((factor, True), jnp.broadcast_to(target, matrix.shape))


def spd_inverse(matrix):
    unit_matrix = jnp.eye(matrix.shape[-1], dtype=matrix.dtype)
    return spd_solve(matrix, unit_matrix)


def on_device(hamilton, coupling, left_contact, right_contact, shifts, coulomb):
    blocks = hamilton.shape[0]
    orbitals = hamilton.shape[-1]
    domain_id = lax.axis_index("domain")
    domain_count = lax.axis_size("domain")
    unit_matrix = jnp.eye(orbitals, dtype=jnp.float32)
    unit_batch = jnp.broadcast_to(unit_matrix, left_contact.shape)
    zero_batch = jnp.zeros_like(left_contact)
    diagonal_blocks = hamilton[None] + shifts[:, None, None, None] * unit_matrix
    first_link = coupling[0]
    contact_term = matmul_hi(matmul_hi(flip(first_link), left_contact), first_link)
    diagonal_blocks = diagonal_blocks.at[:, 0].add(jnp.where(domain_id == 0, contact_term, 0.0))
    diagonal_blocks = diagonal_blocks.at[:, blocks - 1].add(
        jnp.where(domain_id == domain_count - 1, right_contact, 0.0)
    )
    outer_link = jnp.where(domain_id == 0, 0.0, first_link)
    cross = jnp.broadcast_to(outer_link, left_contact.shape)
    inner = diagonal_blocks[:, 0]

    def push_right(incoming):
        return inner - matmul_hi(flip(cross), spd_solve(incoming, cross))

    def push_left(incoming):
        return zero_batch - matmul_hi(cross, spd_solve(inner + incoming, flip(cross)))

    def advance_right(arriving, outgoing):
        return push_right(arriving)

    def advance_left(arriving, outgoing):
        return push_left(arriving)

    def keep_value(arriving, outgoing):
        return outgoing

    def right_turn(sweep_step, carry):
        outgoing, received = carry
        arriving = passed_along(outgoing, "domain", 1)
        my_turn = sweep_step == domain_id
        received = jnp.where(my_turn, arriving, received)
        outgoing = lax.cond(my_turn, advance_right, keep_value, arriving, outgoing)
        return (outgoing, received)

    def left_turn(sweep_step, carry):
        outgoing, received = carry
        arriving = passed_along(outgoing, "domain", -1)
        my_turn = domain_count - 1 - sweep_step == domain_id
        received = jnp.where(my_turn, arriving, received)
        outgoing = lax.cond(my_turn, advance_left, keep_value, arriving, outgoing)
        return (outgoing, received)

    _, from_left = lax.fori_loop(1, domain_count, right_turn, (inner, zero_batch))
    _, right_term = lax.fori_loop(1, domain_count, left_turn, (push_left(zero_batch), zero_batch))
    left_valid = domain_id > 0
    safe_left = jnp.where(left_valid, from_left, unit_batch)
    left_term = jnp.where(
        left_valid, matmul_hi(flip(first_link), spd_solve(safe_left, first_link)), 0.0
    )
    settled = diagonal_blocks.at[:, 0].add(-left_term)
    settled = settled.at[:, blocks - 1].add(right_term)
    left_green = [spd_inverse(settled[:, 0])]
    greens = [left_green[-1]]
    green = jnp.stack(greens, axis=1).astype(jnp.bfloat16)
    elements = lax.all_to_all(green, "energy", split_axis=2, concat_axis=0, tiled=True)
    energies = elements.shape[0]
    columns = elements.reshape(energies, -1).astype(jnp.float32)
    period = 2 * energies
    freq_index = jnp.arange(period, dtype=jnp.int32)
    time_index = jnp.arange(energies, dtype=jnp.int32)
    phase_index = freq_index[:, None] * time_index[None, :] % period
    angles = phase_index.astype(jnp.float32) * (2.0 * math.pi / period)
    cos_table = jnp.cos(angles)
    sin_table = jnp.sin(angles)
    spectrum_real = matmul_hi(cos_table, columns)
    spectrum_imag = -matmul_hi(sin_table, columns)
    power = spectrum_real * spectrum_real + spectrum_imag * spectrum_imag
    polarization = matmul_hi(flip(cos_table), power) / period
    strength = coulomb.reshape(1, -1)
    screened = strength * strength * polarization
    screen_real = matmul_hi(cos_table, screened)
    screen_imag = -matmul_hi(sin_table, screened)
    product_real = spectrum_real * screen_real - spectrum_imag * screen_imag
    product_imag = spectrum_real * screen_imag + spectrum_imag * screen_real
    sigma = (
        matmul_hi(flip(cos_table), product_real) - matmul_hi(flip(sin_table), product_imag)
    ) / period
    sigma = sigma.astype(jnp.bfloat16).reshape(elements.shape)
    return lax.all_to_all(sigma, "energy", split_axis=0, concat_axis=2, tiled=True)


def solution(mesh):
    placed = (
        P("domain", None, None),
        P("domain", None, None),
        P("energy", None, None),
        P("energy", None, None),
        P("energy"),
        P("domain", "energy", None),
    )
    return jax.shard_map(
        on_device,
        mesh=mesh,
        in_specs=placed,
        out_specs=P("energy", "domain", None, None),
        check_vma=False,
    )
```

profile of v0, /device:TPU:1, one launch (start us, length us, event | category | flops | bytes accessed | tf_op | source)
XLA Modules:
  0.0 2344.8 jit_solution(16014596122648640142)
XLA Ops:
  6.5 545.1 %while.54 = (s32[]{:T(128)}, f32[1,256,256]{1,2,0:T(8,128)}, f32[1,256,256]{1,2,0:T(8,128)S(1)}, s32[]{:T(128)}, f32[1,256,256]{2,1,0:T(8,128)S(1)}, /*index=5*/f32[1,256,256]{1,2,0:T(8,128)S(1)}, s32[]{:T(128)}, s32[]{:T(128)}) while((s32[]{:T(128)}, f32[1,256,256]{1,2,0:T(8,128)}, f32[1,256,256]{1,2,0:T(8,128)S(1)}, s32[]{:T(128)}, ...), condition=%wide.region_7.10_spmd.clone, body=%wide.region_0.9_spmd.clone.sunk | while | flops 554582272 | bytes 8325509 | solution.py:83
  15.0 68.4 %collective-permute-start.1 = (f32[1,256,256]{1,2,0:T(8,128)}, f32[1,256,256]{1,2,0:T(8,128)S(1)}, u32[]{:S(2)}, u32[]{:S(2)}) collective-permute-start(f32[1,256,256]{1,2,0:T(8,128)} %get-tuple-element.871), channel_id=1, source_target_pairs={{0,1},{1,2},{2,3},{3,4},{4,5},{5,6},{6,7},{7,8},{8,9},{9,10},{10,1... | collective-permute-start | bytes 786440 | tf_op jit(solution)/shard_map/while/body/eval_jaxpr/ppermute | solution.py:12
  94.6 64.5 %collective-permute-start.1 = (f32[1,256,256]{1,2,0:T(8,128)}, f32[1,256,256]{1,2,0:T(8,128)S(1)}, u32[]{:S(2)}, u32[]{:S(2)}) collective-permute-start(f32[1,256,256]{1,2,0:T(8,128)} %get-tuple-element.871), channel_id=1, source_target_pairs={{0,1},{1,2},{2,3},{3,4},{4,5},{5,6},{6,7},{7,8},{8,9},{9,10},{10,1... | collective-permute-start | bytes 786440 | tf_op jit(solution)/shard_map/while/body/eval_jaxpr/ppermute | solution.py:12
  170.2 64.6 %collective-permute-start.1 = (f32[1,256,256]{1,2,0:T(8,128)}, f32[1,256,256]{1,2,0:T(8,128)S(1)}, u32[]{:S(2)}, u32[]{:S(2)}) collective-permute-start(f32[1,256,256]{1,2,0:T(8,128)} %get-tuple-element.871), channel_id=1, source_target_pairs={{0,1},{1,2},{2,3},{3,4},{4,5},{5,6},{6,7},{7,8},{8,9},{9,10},{10,1... | collective-permute-start | bytes 786440 | tf_op jit(solution)/shard_map/while/body/eval_jaxpr/ppermute | solution.py:12
  246.0 65.8 %collective-permute-start.1 = (f32[1,256,256]{1,2,0:T(8,128)}, f32[1,256,256]{1,2,0:T(8,128)S(1)}, u32[]{:S(2)}, u32[]{:S(2)}) collective-permute-start(f32[1,256,256]{1,2,0:T(8,128)} %get-tuple-element.871), channel_id=1, source_target_pairs={{0,1},{1,2},{2,3},{3,4},{4,5},{5,6},{6,7},{7,8},{8,9},{9,10},{10,1... | collective-permute-start | bytes 786440 | tf_op jit(solution)/shard_map/while/body/eval_jaxpr/ppermute | solution.py:12
  324.1 63.4 %collective-permute-start.1 = (f32[1,256,256]{1,2,0:T(8,128)}, f32[1,256,256]{1,2,0:T(8,128)S(1)}, u32[]{:S(2)}, u32[]{:S(2)}) collective-permute-start(f32[1,256,256]{1,2,0:T(8,128)} %get-tuple-element.871), channel_id=1, source_target_pairs={{0,1},{1,2},{2,3},{3,4},{4,5},{5,6},{6,7},{7,8},{8,9},{9,10},{10,1... | collective-permute-start | bytes 786440 | tf_op jit(solution)/shard_map/while/body/eval_jaxpr/ppermute | solution.py:12
  399.8 63.4 %collective-permute-start.1 = (f32[1,256,256]{1,2,0:T(8,128)}, f32[1,256,256]{1,2,0:T(8,128)S(1)}, u32[]{:S(2)}, u32[]{:S(2)}) collective-permute-start(f32[1,256,256]{1,2,0:T(8,128)} %get-tuple-element.871), channel_id=1, source_target_pairs={{0,1},{1,2},{2,3},{3,4},{4,5},{5,6},{6,7},{7,8},{8,9},{9,10},{10,1... | collective-permute-start | bytes 786440 | tf_op jit(solution)/shard_map/while/body/eval_jaxpr/ppermute | solution.py:12
  475.6 63.4 %collective-permute-start.1 = (f32[1,256,256]{1,2,0:T(8,128)}, f32[1,256,256]{1,2,0:T(8,128)S(1)}, u32[]{:S(2)}, u32[]{:S(2)}) collective-permute-start(f32[1,256,256]{1,2,0:T(8,128)} %get-tuple-element.871), channel_id=1, source_target_pairs={{0,1},{1,2},{2,3},{3,4},{4,5},{5,6},{6,7},{7,8},{8,9},{9,10},{10,1... | collective-permute-start | bytes 786440 | tf_op jit(solution)/shard_map/while/body/eval_jaxpr/ppermute | solution.py:12
  552.1 11.7 custom-call.41
  574.3 11.7 custom-call.43
  592.3 19.9 custom-call.44
  614.7 11.7 custom-call.45
  637.0 11.7 custom-call.47
  654.8 20.1 custom-call.48
  677.3 1529.8 %while.55 = (s32[]{:T(128)}, f32[1,256,256]{1,2,0:T(8,128)S(1)}, f32[1,256,256]{1,2,0:T(8,128)S(1)}, s32[]{:T(128)}, f32[1,256,256]{1,2,0:T(8,128)S(1)}, /*index...) while((s32[]{:T(128)}, f32[1,256,256]{1,2,0:T(8,128)S(1)}, ...), condition=%wide.region_11.14_spmd.clone, body=%wide.region_8.0_spmd.clone.sunk | while | flops 554647808 | bytes 8849833 | solution.py:84
  678.6 67.1 %collective-permute-done = f32[1,256,256]{1,2,0:T(8,128)S(1)} collective-permute-done((f32[1,256,256]{1,2,0:T(8,128)S(1)}, f32[1,256,256]{1,2,0:T(8,128)S(1)}, u32[]{:S(2)}, u32[]{:S(2)}) %collective-permute-start) | collective-permute-done | bytes 262176 | tf_op jit(solution)/shard_map/while/body/eval_jaxpr/ppermute | solution.py:12
  755.8 65.9 %collective-permute-done = f32[1,256,256]{1,2,0:T(8,128)S(1)} collective-permute-done((f32[1,256,256]{1,2,0:T(8,128)S(1)}, f32[1,256,256]{1,2,0:T(8,128)S(1)}, u32[]{:S(2)}, u32[]{:S(2)}) %collective-permute-start) | collective-permute-done | bytes 262176 | tf_op jit(solution)/shard_map/while/body/eval_jaxpr/ppermute | solution.py:12
  831.8 65.8 %collective-permute-done = f32[1,256,256]{1,2,0:T(8,128)S(1)} collective-permute-done((f32[1,256,256]{1,2,0:T(8,128)S(1)}, f32[1,256,256]{1,2,0:T(8,128)S(1)}, u32[]{:S(2)}, u32[]{:S(2)}) %collective-permute-start) | collective-permute-done | bytes 262176 | tf_op jit(solution)/shard_map/while/body/eval_jaxpr/ppermute | solution.py:12
  907.8 65.8 %collective-permute-done = f32[1,256,256]{1,2,0:T(8,128)S(1)} collective-permute-done((f32[1,256,256]{1,2,0:T(8,128)S(1)}, f32[1,256,256]{1,2,0:T(8,128)S(1)}, u32[]{:S(2)}, u32[]{:S(2)}) %collective-permute-start) | collective-permute-done | bytes 262176 | tf_op jit(solution)/shard_map/while/body/eval_jaxpr/ppermute | solution.py:12
  983.8 67.0 %collective-permute-done = f32[1,256,256]{1,2,0:T(8,128)S(1)} collective-permute-done((f32[1,256,256]{1,2,0:T(8,128)S(1)}, f32[1,256,256]{1,2,0:T(8,128)S(1)}, u32[]{:S(2)}, u32[]{:S(2)}) %collective-permute-start) | collective-permute-done | bytes 262176 | tf_op jit(solution)/shard_map/while/body/eval_jaxpr/ppermute | solution.py:12
  1061.0 65.8 %collective-permute-done = f32[1,256,256]{1,2,0:T(8,128)S(1)} collective-permute-done((f32[1,256,256]{1,2,0:T(8,128)S(1)}, f32[1,256,256]{1,2,0:T(8,128)S(1)}, u32[]{:S(2)}, u32[]{:S(2)}) %collective-permute-start) | collective-permute-done | bytes 262176 | tf_op jit(solution)/shard_map/while/body/eval_jaxpr/ppermute | solution.py:12
  1137.0 65.8 %collective-permute-done = f32[1,256,256]{1,2,0:T(8,128)S(1)} collective-permute-done((f32[1,256,256]{1,2,0:T(8,128)S(1)}, f32[1,256,256]{1,2,0:T(8,128)S(1)}, u32[]{:S(2)}, u32[]{:S(2)}) %collective-permute-start) | collective-permute-done | bytes 262176 | tf_op jit(solution)/shard_map/while/body/eval_jaxpr/ppermute | solution.py:12
  1212.7 932.2 %collective-permute-done = f32[1,256,256]{1,2,0:T(8,128)S(1)} collective-permute-done((f32[1,256,256]{1,2,0:T(8,128)S(1)}, f32[1,256,256]{1,2,0:T(8,128)S(1)}, u32[]{:S(2)}, u32[]{:S(2)}) %collective-permute-start) | collective-permute-done | bytes 262176 | tf_op jit(solution)/shard_map/while/body/eval_jaxpr/ppermute | solution.py:12
  2144.9 61.9 %conditional.7 = (f32[1,256,256]{1,2,0:T(8,128)S(1)}) conditional(s32[]{:T(128)} %convert_element_type.97, f32[1,256,256]{1,2,0:T(8,128)S(1)} %get-tuple-element.843, (f32[1,256,256]{1,2,0:T(8,128)S(1)}, f32[1,256,256]{1,2,0:T(8,128)S(1)}, f32[1,256,256]{1,2,0:T(8,128)S(1)}, f32[256,256]{1,0:T(8,128)S(1)}) %tuple.188), branch_computations={%region_9.11_spmd, %region_10.12_spmd} | conditional | flops 554516736 | bytes 7014607 | solution.py:80
  2145.1 11.7 custom-call.37
  2167.2 11.7 custom-call.39
  2184.7 19.7 custom-call.40
  2207.9 11.7 custom-call.49
  2229.9 11.7 custom-call.51
  2248.4 19.9 custom-call.52
  2273.0 39.1 %all-to-all-start = ((bf16[64,2,512]{2,1,0:T(2,128)(2,1)}), bf16[64,2,512]{2,1,0:T(2,128)(2,1)S(1)}, u32[]{:S(2)}, u32[]{:S(2)}) async-start(bf16[64,2,512]{2,1,0:T(2,128)(2,1)} %reshape.387), calls=%async_computation | async-start | bytes 262144 | tf_op jit(solution)/shard_map/all_to_all | solution.py:95
  2328.6 15.1 all_to_all.21
  (264 shorter events, 275.7 us)
Async XLA Ops:
  6.5 8.4 collective-permute-start.1
  15.0 72.0 %collective-permute-start.1 = (f32[1,256,256]{1,2,0:T(8,128)}, f32[1,256,256]{1,2,0:T(8,128)S(1)}, u32[]{:S(2)}, u32[]{:S(2)}) collective-permute-start(f32[1,256,256]{1,2,0:T(8,128)} %get-tuple-element.871), channel_id=1, source_target_pairs={{0,1},{1,2},{2,3},{3,4},{4,5},{5,6},{6,7},{7,8},{8,9},{9,10},{10,1... | collective-permute-start | bytes 786440 | tf_op jit(solution)/shard_map/while/body/eval_jaxpr/ppermute | solution.py:12
  87.1 7.5 collective-permute-start.1
  94.6 68.1 %collective-permute-start.1 = (f32[1,256,256]{1,2,0:T(8,128)}, f32[1,256,256]{1,2,0:T(8,128)S(1)}, u32[]{:S(2)}, u32[]{:S(2)}) collective-permute-start(f32[1,256,256]{1,2,0:T(8,128)} %get-tuple-element.871), channel_id=1, source_target_pairs={{0,1},{1,2},{2,3},{3,4},{4,5},{5,6},{6,7},{7,8},{8,9},{9,10},{10,1... | collective-permute-start | bytes 786440 | tf_op jit(solution)/shard_map/while/body/eval_jaxpr/ppermute | solution.py:12
  162.8 7.3 collective-permute-start.1
  170.2 68.2 %collective-permute-start.1 = (f32[1,256,256]{1,2,0:T(8,128)}, f32[1,256,256]{1,2,0:T(8,128)S(1)}, u32[]{:S(2)}, u32[]{:S(2)}) collective-permute-start(f32[1,256,256]{1,2,0:T(8,128)} %get-tuple-element.871), channel_id=1, source_target_pairs={{0,1},{1,2},{2,3},{3,4},{4,5},{5,6},{6,7},{7,8},{8,9},{9,10},{10,1... | collective-permute-start | bytes 786440 | tf_op jit(solution)/shard_map/while/body/eval_jaxpr/ppermute | solution.py:12
  238.5 7.3 collective-permute-start.1
  246.0 69.4 %collective-permute-start.1 = (f32[1,256,256]{1,2,0:T(8,128)}, f32[1,256,256]{1,2,0:T(8,128)S(1)}, u32[]{:S(2)}, u32[]{:S(2)}) collective-permute-start(f32[1,256,256]{1,2,0:T(8,128)} %get-tuple-element.871), channel_id=1, source_target_pairs={{0,1},{1,2},{2,3},{3,4},{4,5},{5,6},{6,7},{7,8},{8,9},{9,10},{10,1... | collective-permute-start | bytes 786440 | tf_op jit(solution)/shard_map/while/body/eval_jaxpr/ppermute | solution.py:12
  315.5 8.5 collective-permute-start.1
  324.1 67.0 %collective-permute-start.1 = (f32[1,256,256]{1,2,0:T(8,128)}, f32[1,256,256]{1,2,0:T(8,128)S(1)}, u32[]{:S(2)}, u32[]{:S(2)}) collective-permute-start(f32[1,256,256]{1,2,0:T(8,128)} %get-tuple-element.871), channel_id=1, source_target_pairs={{0,1},{1,2},{2,3},{3,4},{4,5},{5,6},{6,7},{7,8},{8,9},{9,10},{10,1... | collective-permute-start | bytes 786440 | tf_op jit(solution)/shard_map/while/body/eval_jaxpr/ppermute | solution.py:12
  391.2 8.5 collective-permute-start.1
  399.8 67.0 %collective-permute-start.1 = (f32[1,256,256]{1,2,0:T(8,128)}, f32[1,256,256]{1,2,0:T(8,128)S(1)}, u32[]{:S(2)}, u32[]{:S(2)}) collective-permute-start(f32[1,256,256]{1,2,0:T(8,128)} %get-tuple-element.871), channel_id=1, source_target_pairs={{0,1},{1,2},{2,3},{3,4},{4,5},{5,6},{6,7},{7,8},{8,9},{9,10},{10,1... | collective-permute-start | bytes 786440 | tf_op jit(solution)/shard_map/while/body/eval_jaxpr/ppermute | solution.py:12
  466.9 8.5 collective-permute-start.1
  475.6 67.0 %collective-permute-start.1 = (f32[1,256,256]{1,2,0:T(8,128)}, f32[1,256,256]{1,2,0:T(8,128)S(1)}, u32[]{:S(2)}, u32[]{:S(2)}) collective-permute-start(f32[1,256,256]{1,2,0:T(8,128)} %get-tuple-element.871), channel_id=1, source_target_pairs={{0,1},{1,2},{2,3},{3,4},{4,5},{5,6},{6,7},{7,8},{8,9},{9,10},{10,1... | collective-permute-start | bytes 786440 | tf_op jit(solution)/shard_map/while/body/eval_jaxpr/ppermute | solution.py:12
  542.6 8.5 collective-permute-start.1
  677.3 68.4 %collective-permute-start = (f32[1,256,256]{1,2,0:T(8,128)S(1)}, f32[1,256,256]{1,2,0:T(8,128)S(1)}, u32[]{:S(2)}, u32[]{:S(2)}) collective-permute-start(f32[1,256,256]{1,2,0:T(8,128)S(1)} %get-tuple-element.843), channel_id=1, source_target_pairs={{1,0},{2,1},{3,2},{4,3},{5,4},{6,5},{7,6},{8,7},{9,8},{10,9},{11,1... | collective-permute-start | bytes 786440 | tf_op jit(solution)/shard_map/while/body/eval_jaxpr/ppermute | solution.py:12
  745.8 8.7 collective-permute-start
  754.5 67.2 %collective-permute-start = (f32[1,256,256]{1,2,0:T(8,128)S(1)}, f32[1,256,256]{1,2,0:T(8,128)S(1)}, u32[]{:S(2)}, u32[]{:S(2)}) collective-permute-start(f32[1,256,256]{1,2,0:T(8,128)S(1)} %get-tuple-element.843), channel_id=1, source_target_pairs={{1,0},{2,1},{3,2},{4,3},{5,4},{6,5},{7,6},{8,7},{9,8},{10,9},{11,1... | collective-permute-start | bytes 786440 | tf_op jit(solution)/shard_map/while/body/eval_jaxpr/ppermute | solution.py:12
  821.8 8.7 collective-permute-start
  830.5 67.1 %collective-permute-start = (f32[1,256,256]{1,2,0:T(8,128)S(1)}, f32[1,256,256]{1,2,0:T(8,128)S(1)}, u32[]{:S(2)}, u32[]{:S(2)}) collective-permute-start(f32[1,256,256]{1,2,0:T(8,128)S(1)} %get-tuple-element.843), channel_id=1, source_target_pairs={{1,0},{2,1},{3,2},{4,3},{5,4},{6,5},{7,6},{8,7},{9,8},{10,9},{11,1... | collective-permute-start | bytes 786440 | tf_op jit(solution)/shard_map/while/body/eval_jaxpr/ppermute | solution.py:12
  897.8 8.7 collective-permute-start
  906.5 67.2 %collective-permute-start = (f32[1,256,256]{1,2,0:T(8,128)S(1)}, f32[1,256,256]{1,2,0:T(8,128)S(1)}, u32[]{:S(2)}, u32[]{:S(2)}) collective-permute-start(f32[1,256,256]{1,2,0:T(8,128)S(1)} %get-tuple-element.843), channel_id=1, source_target_pairs={{1,0},{2,1},{3,2},{4,3},{5,4},{6,5},{7,6},{8,7},{9,8},{10,9},{11,1... | collective-permute-start | bytes 786440 | tf_op jit(solution)/shard_map/while/body/eval_jaxpr/ppermute | solution.py:12
  973.7 8.7 collective-permute-start
  982.5 68.4 %collective-permute-start = (f32[1,256,256]{1,2,0:T(8,128)S(1)}, f32[1,256,256]{1,2,0:T(8,128)S(1)}, u32[]{:S(2)}, u32[]{:S(2)}) collective-permute-start(f32[1,256,256]{1,2,0:T(8,128)S(1)} %get-tuple-element.843), channel_id=1, source_target_pairs={{1,0},{2,1},{3,2},{4,3},{5,4},{6,5},{7,6},{8,7},{9,8},{10,9},{11,1... | collective-permute-start | bytes 786440 | tf_op jit(solution)/shard_map/while/body/eval_jaxpr/ppermute | solution.py:12
  1050.9 8.7 collective-permute-start
  1059.7 67.2 %collective-permute-start = (f32[1,256,256]{1,2,0:T(8,128)S(1)}, f32[1,256,256]{1,2,0:T(8,128)S(1)}, u32[]{:S(2)}, u32[]{:S(2)}) collective-permute-start(f32[1,256,256]{1,2,0:T(8,128)S(1)} %get-tuple-element.843), channel_id=1, source_target_pairs={{1,0},{2,1},{3,2},{4,3},{5,4},{6,5},{7,6},{8,7},{9,8},{10,9},{11,1... | collective-permute-start | bytes 786440 | tf_op jit(solution)/shard_map/while/body/eval_jaxpr/ppermute | solution.py:12
  1127.0 8.7 collective-permute-start
  1135.7 67.1 %collective-permute-start = (f32[1,256,256]{1,2,0:T(8,128)S(1)}, f32[1,256,256]{1,2,0:T(8,128)S(1)}, u32[]{:S(2)}, u32[]{:S(2)}) collective-permute-start(f32[1,256,256]{1,2,0:T(8,128)S(1)} %get-tuple-element.843), channel_id=1, source_target_pairs={{1,0},{2,1},{3,2},{4,3},{5,4},{6,5},{7,6},{8,7},{9,8},{10,9},{11,1... | collective-permute-start | bytes 786440 | tf_op jit(solution)/shard_map/while/body/eval_jaxpr/ppermute | solution.py:12
  1202.9 8.3 collective-permute-start
  1211.3 933.5 %collective-permute-start = (f32[1,256,256]{1,2,0:T(8,128)S(1)}, f32[1,256,256]{1,2,0:T(8,128)S(1)}, u32[]{:S(2)}, u32[]{:S(2)}) collective-permute-start(f32[1,256,256]{1,2,0:T(8,128)S(1)} %get-tuple-element.843), channel_id=1, source_target_pairs={{1,0},{2,1},{3,2},{4,3},{5,4},{6,5},{7,6},{8,7},{9,8},{10,9},{11,1... | collective-permute-start | bytes 786440 | tf_op jit(solution)/shard_map/while/body/eval_jaxpr/ppermute | solution.py:12
  2273.0 39.2 %copy-start.6 = (f32[1,4,256]{2,1,0:T(4,128)S(1)}, f32[1,4,256]{2,1,0:T(4,128)}, u32[]{:S(2)}) copy-start(f32[1,4,256]{2,1,0:T(4,128)} %param.30) | copy-start | bytes 12292
  2273.0 49.6 %all-to-all-start = ((bf16[64,2,512]{2,1,0:T(2,128)(2,1)}), bf16[64,2,512]{2,1,0:T(2,128)(2,1)S(1)}, u32[]{:S(2)}, u32[]{:S(2)}) async-start(bf16[64,2,512]{2,1,0:T(2,128)(2,1)} %reshape.387), calls=%async_computation | async-start | bytes 262144 | tf_op jit(solution)/shard_map/all_to_all | solution.py:95
  (6 other events, 44.2 us)
where the time goes:
time: 2360 us; the launch traced here: 2340 us
  waiting for transfers between devices  1510 us (64%)
  starting transfers between devices  548 us (23%)
  other arithmetic  222 us (9%)
    ppermute x30, waiting for transfers between devices, passed_along(): return lax.ppermute(array, axis, pairs)  1500 us
    ppermute x30, starting transfers between devices, passed_along(): return lax.ppermute(array, axis, pairs)  509 us
    another operation x25, other arithmetic, spd_solve(): factor = jnp.linalg.cholesky(matrix)  137 us
    another operation x11, other arithmetic, spd_solve(): jax.scipy.linalg.cho_solve((factor, True), jnp.broadcast_to(target, matri...  79.6 us
  transfers between devices with their start and end apart: 31, of which 31 were waited for; matrix products, arithmetic and copies ran while one was open for 0% of the time, Pallas kernels for 0%

commit v1 on v0

v1 whole, which is shorter than its diff:
```python
import functools

import jax
import jax.numpy as jnp
from jax import lax
from jax.experimental import pallas as pl
from jax.experimental.pallas import tpu as pltpu
from jax.sharding import PartitionSpec as P

ORB = 256
HALF = ORB // 2
ROWS = 8
HIGHEST = lax.Precision.HIGHEST
VMEM = pl.BlockSpec(memory_space=pltpu.VMEM)
SMEM = pl.BlockSpec(memory_space=pltpu.SMEM)
PACKED = ORB + ROWS


def dot(left, right, left_dim=1, right_dim=0):
    return lax.dot_general(
        left, right, (((left_dim,), (right_dim,)), ((), ())),
        precision=HIGHEST, preferred_element_type=jnp.float32,
    )


def eliminated_panel(rows, first):
    width = rows.shape[1]
    lane = lax.broadcasted_iota(jnp.int32, rows.shape, 1)
    sublane = lax.broadcasted_iota(jnp.int32, rows.shape, 0)
    spread = [jnp.broadcast_to(rows[:, first + j:first + j + 1], (ROWS, width)) for j in range(ROWS)]
    for k in range(ROWS):
        factor = spread[k]
        scale = 1.0 / factor[k:k + 1, :]
        is_pivot = sublane == k
        for j in range(k + 1, ROWS):
            scaled = spread[j][k:k + 1, :] * scale
            spread[j] = jnp.where(is_pivot, scaled, spread[j] - factor * scaled)
        own_column = lane == first + k
        pivot_row = jnp.where(own_column[:1], 1.0, rows[k:k + 1, :]) * scale
        rows = jnp.where(is_pivot, pivot_row, jnp.where(own_column, 0.0, rows) - factor * pivot_row)
    return rows


def inverse_half(matrix):
    size = matrix.shape[0]
    count = size // ROWS
    lane = lax.broadcasted_iota(jnp.int32, (ROWS, size), 1)
    groups = [matrix[ROWS * i:ROWS * i + ROWS, :] for i in range(count)]
    for t in range(count):
        first = ROWS * t
        pivots = eliminated_panel(groups[t], first)
        groups[t] = pivots
        own = (lane >= first) & (lane < first + ROWS)
        for i in [(t + 1 + i) % count for i in range(count - 1)]:
            rows = groups[i]
            update = rows[:, first:first + 1] * pivots[0:1, :]
            for j in range(1, ROWS):
                update = update + rows[:, first + j:first + j + 1] * pivots[j:j + 1, :]
            groups[i] = jnp.where(own, 0.0, rows) - update
    return jnp.concatenate(groups, axis=0)


def half_indices():
    row = lax.broadcasted_iota(jnp.int32, (HALF, HALF), 0)
    column = lax.broadcasted_iota(jnp.int32, (HALF, HALF), 1)
    return row, column


def pack(matrix, out):
    row, column = half_indices()
    low = matrix[HALF:, HALF:]
    out[:HALF] = matrix[:HALF, HALF:]
    out[HALF:ORB] = jnp.where(row <= column, matrix[:HALF, :HALF], low)
    diagonal = jnp.sum(jnp.where(row == column, low, 0.0), axis=0, keepdims=True)
    out[ORB:] = jnp.broadcast_to(diagonal, (ROWS, HALF))


def unpack(packed):
    row, column = half_indices()
    corner = packed[:HALF]
    both = packed[HALF:ORB]
    turned = both.T
    top = jnp.where(row <= column, both, turned)
    low = jnp.where(row > column, both, turned)
    low = jnp.where(row == column, packed[ORB:ORB + 1], low)
    return jnp.concatenate(
        [jnp.concatenate([top, corner], axis=1), jnp.concatenate([corner.T, low], axis=1)], axis=0
    )


def message(source, target, send, recv, to, axis="domain"):
    return pltpu.make_async_remote_copy(
        src_ref=source, dst_ref=target, send_sem=send, recv_sem=recv,
        device_id={axis: to}, device_id_type=pl.DeviceIdType.MESH,
    )


CHUNKS = ((0, 64), (64, 64), (128, 64), (192, 72))


def chain_kernel(
    shift, hamilton, coupling, left_contact, right_contact, coulomb, out,
    block, matrix, inverse, part, part_inverse, solved, lead, side,
    ups, downs, links, toward, away, longer, across,
    to_ring, from_ring, to_pair, from_pair, to_middle, middle, settled, opposite,
    green, padded, screened, result, arrived,
    load_sem, send_sem, recv_sem, pair_sem, near_sem, far_sem, spread_sem,
):
    place = lax.axis_index("domain")
    count = lax.axis_size("domain")
    me = lax.axis_index("energy")
    energies = green.shape[0]
    quarter = place // 4
    inner = (place >= 4) & (place < 12)
    odd = lax.rem(quarter, 2)
    even = odd == 0
    pair, near, far = place + 4 - 8 * odd, place + 12 - 8 * quarter, lax.rem(place + 8, count)
    loads = [
        pltpu.make_async_copy(source.at[0], target, load_sem.at[i])
        for i, (source, target) in enumerate(
            ((hamilton, block), (coupling, ups.at[0]), (left_contact, lead), (right_contact, side))
        )
    ]
    for load in loads:
        load.start()

    def neighbour(by):
        return lax.rem(place + by + count, count)

    def other(k):
        return lax.rem(me + k, energies)

    peers = [neighbour(1), neighbour(-1), neighbour(2), neighbour(-2), pair, near, far]
    barrier = pltpu.get_barrier_semaphore()
    for peer in peers:
        pl.semaphore_signal(barrier, inc=1, device_id={"domain": peer}, device_id_type=pl.DeviceIdType.MESH)

    def greet(k, carry):
        pl.semaphore_signal(barrier, inc=1, device_id={"energy": other(k)}, device_id_type=pl.DeviceIdType.MESH)
        return carry

    lax.fori_loop(1, energies, greet, 0)
    first_link = message(coupling.at[0], downs.at[0], send_sem.at[0], recv_sem.at[0], neighbour(-1))

    def ring_messages(turn):
        stride = turn + 1
        left, right = neighbour(-stride), neighbour(stride)
        base = 1 + 4 * turn
        return [
            message(to_ring.at[turn, 0], from_ring.at[turn, 0], send_sem.at[base], recv_sem.at[base], left),
            message(to_ring.at[turn, 1], from_ring.at[turn, 1], send_sem.at[base + 1], recv_sem.at[base + 1], right),
            message(links.at[turn], downs.at[turn + 1], send_sem.at[base + 2], recv_sem.at[base + 2], left),
            message(links.at[turn], ups.at[turn + 1], send_sem.at[base + 3], recv_sem.at[base + 3], right),
        ]

    def chunk_messages(source, target, send, recv, to):
        return [
            message(source.at[pl.ds(*rows)], target.at[pl.ds(*rows)], send.at[i], recv.at[i], to)
            for i, rows in enumerate(CHUNKS)
        ]

    pair_messages = chunk_messages(to_pair, from_pair, pair_sem.at[0], pair_sem.at[1], pair)
    near_messages = chunk_messages(settled, opposite, near_sem.at[0], near_sem.at[1], near)
    far_messages = chunk_messages(settled, opposite, far_sem.at[0], near_sem.at[1], far)
    middle_message = message(to_middle, middle, send_sem.at[9], recv_sem.at[9], pair)
    link_message = message(longer, across, send_sem.at[10], recv_sem.at[10], pair)

    def before_first():
        for load in loads:
            load.wait()
        row = lax.broadcasted_iota(jnp.int32, (ORB, ORB), 0)
        column = lax.broadcasted_iota(jnp.int32, (ORB, ORB), 1)
        block[...] += jnp.where(row == column, shift[0], 0.0)

        @pl.when(place == 0)
        def _():
            link = ups[0]
            block[...] += dot(link, dot(lead[...], link), 0, 0)
            ups[0] = jnp.zeros((ORB, ORB), jnp.float32)

        @pl.when(place == count - 1)
        def _():
            block[...] += side[...]

        matrix[...] = block[...]

    def before_ring(turn):
        messages = ring_messages(turn)
        messages[0].wait_recv()
        messages[1].wait_recv()

        @pl.when(turn == 0)
        def _():
            left_inverse = unpack(from_ring[turn, 1])
            block[...] -= dot(ups[0], dot(left_inverse, ups[0]), 0, 0)

        @pl.when(turn == 1)
        def _():
            block[...] -= unpack(from_ring[turn, 1])

        block[...] -= unpack(from_ring[turn, 0])
        matrix[...] = block[...]

    def before_middle():
        @pl.when(inner)
        def _():
            pack(block[...], settled)
            for i, rows in enumerate(CHUNKS):
                pair_messages[i].wait_recv()
                settled[pl.ds(*rows)] -= from_pair[pl.ds(*rows)]
                far_messages[i].start()
                near_messages[i].start()
            block[...] = unpack(settled[...])
            for received in near_messages:
                received.wait_recv()
            matrix[...] = unpack(opposite[...])

        @pl.when(jnp.logical_not(inner))
        def _():
            for received in pair_messages:
                received.wait_recv()
            block[...] -= unpack(from_pair[...])
            middle_message.wait_recv()
            for received in far_messages:
                received.wait_recv()
            matrix[...] = unpack(opposite[...] - middle[...])

    def before_last():
        @pl.when(inner)
        def _():
            across[...] = away[...].T

        @pl.when(jnp.logical_not(inner))
        def _():
            link_message.wait_recv()

        link = across[...]
        block[...] -= dot(link, dot(inverse[...], link), 0, 0)
        matrix[...] = block[...]

    def after_ring(turn):
        messages = ring_messages(turn)

        @pl.when(turn == 0)
        def _():
            pack(inverse[...], to_ring.at[turn, 1])
            messages[1].start()

        @pl.when(turn == 1)
        def _():
            for received in ring_messages(0)[2:]:
                received.wait_recv()

        pack(dot(ups[turn], dot(inverse[...], ups[turn], 1, 1)), to_ring.at[turn, 0])
        messages[0].start()

        @pl.when(turn == 0)
        def _():
            first_link.wait_recv()

            @pl.when(place == count - 1)
            def _():
                downs[0] = jnp.zeros((ORB, ORB), jnp.float32)

        matrix[...] = dot(inverse[...], downs[turn])

        @pl.when(turn == 1)
        def _():
            pack(dot(downs[turn], matrix[...], 0, 0), to_ring.at[turn, 1])
            messages[1].start()

        links[turn] = -dot(ups[turn], matrix[...])
        messages[2].start()
        messages[3].start()

    def after_pair():
        for received in ring_messages(1)[2:]:
            received.wait_recv()
        turned = ups[2].T
        toward[...] = jnp.where(even, downs[2], turned)
        pack(dot(toward[...], dot(inverse[...], toward[...]), 0, 0), to_pair)
        for sent in pair_messages:
            sent.start()
        away[...] = jnp.where(even, turned, downs[2])

        @pl.when(inner)
        def _():
            matrix[...] = dot(inverse[...], away[...])
            pack(dot(away[...], matrix[...], 0, 0), to_middle)
            middle_message.start()
            longer[...] = -dot(matrix[...], toward[...], 0, 0)
            link_message.start()

    def turn_half(step, carry):
        turn, half = step // 2, lax.rem(step, 2)

        @pl.when(step == 1)
        def _():
            pl.semaphore_wait(barrier, len(peers) + energies - 1)
            first_link.start()

        @pl.when(half == 0)
        def _():
            pl.when(turn == 0)(before_first)
            pl.when((turn == 1) | (turn == 2))(lambda: before_ring(turn - 1))
            pl.when(turn == 3)(before_middle)
            pl.when(turn == 4)(before_last)
            part[...] = matrix[:HALF, :HALF]

        @pl.when(half == 1)
        def _():
            top = part_inverse[...]
            corner = matrix[:HALF, HALF:]
            inverse[:HALF, :HALF] = top
            solved[...] = dot(top, corner)
            part[...] = matrix[HALF:, HALF:] - dot(corner, solved[...], 0, 0)

        part_inverse[...] = inverse_half(part[...])

        @pl.when(half == 1)
        def _():
            low = part_inverse[...]
            corner = dot(solved[...], low)
            inverse[:HALF, :HALF] += dot(corner, solved[...], 1, 1)
            inverse[:HALF, HALF:] = -corner
            inverse[HALF:, :HALF] = -corner.T
            inverse[HALF:, HALF:] = low
            pl.when(turn <= 1)(lambda: after_ring(turn))
            pl.when(turn == 2)(after_pair)

        return carry

    lax.fori_loop(0, 10, turn_half, 0)
    for e in range(energies):
        rows = inverse[4 * e:4 * e + 4, :]
        tile = jnp.concatenate([rows[:, :HALF], rows[:, HALF:]], axis=0)
        green[e] = tile.astype(jnp.bfloat16).astype(jnp.float32)

    def exchange(source, target, offset, index):
        own = pltpu.make_async_copy(source.at[me], target.at[offset + me], load_sem.at[4 + index])
        own.start()

        def send(k, carry):
            to = other(k)
            message(
                source.at[to], target.at[offset + me], spread_sem.at[0, index], spread_sem.at[1, index], to, "energy",
            ).start()
            return carry

        lax.fori_loop(1, energies, send, 0)
        return own, message(
            source.at[pl.ds(0, energies - 1)], target.at[pl.ds(offset, energies - 1)],
            spread_sem.at[0, index], spread_sem.at[1, index], other(1), "energy",
        )

    own, rest = exchange(green, padded, 8, 0)
    padded[:8] = jnp.zeros((8, ROWS, HALF), jnp.float32)
    padded[8 + energies:] = jnp.zeros((8, ROWS, HALF), jnp.float32)
    factor = jnp.concatenate([coulomb[0, :, :HALF], coulomb[0, :, HALF:]], axis=0)
    factor = factor * factor
    first_link.wait_send()
    for turn in range(2):
        for sent in ring_messages(turn):
            sent.wait_send()
    for sent in pair_messages:
        sent.wait_send()

    @pl.when(inner)
    def _():
        for sent in (middle_message, link_message, *near_messages, *far_messages):
            sent.wait_send()

    own.wait()
    rest.wait()
    blocks = energies // 8
    for kb in range(blocks):
        sums = [None] * 8
        for jb in range(blocks - kb):
            base = [padded[8 + 8 * jb + a] for a in range(8)]
            ahead = [padded[8 + 8 * (jb + kb) + c] for c in range(15)]
            for b in range(8):
                for a in range(8):
                    term = base[a] * ahead[a + b]
                    sums[b] = term if sums[b] is None else sums[b] + term
        for b in range(8):
            screened[8 * kb + b] = factor * sums[b]
    for kb in range(blocks):
        sums = [None] * 8
        for jb in range(kb + 1):
            base = [screened[8 * jb + a] for a in range(8)]
            behind = [padded[8 + 8 * (kb - jb) + c - 7] for c in range(15)]
            for b in range(8):
                for a in range(8):
                    term = base[a] * behind[b - a + 7]
                    sums[b] = term if sums[b] is None else sums[b] + term
        for b in range(8):
            result[8 * kb + b] = sums[b]
    own, rest = exchange(result, arrived, 0, 1)
    own.wait()
    rest.wait()
    for q in range(energies // 4):
        rows = [
            jnp.concatenate([arrived[4 * q + t, :4, :], arrived[4 * q + t, 4:, :]], axis=1) for t in range(4)
        ]
        out[16 * q:16 * q + 16, :] = jnp.concatenate(rows, axis=0).astype(jnp.bfloat16)


TILES = (ORB // 4, ROWS, HALF)


def on_device(hamilton, coupling, left_contact, right_contact, shifts, coulomb):
    def several(*shape):
        return pltpu.VMEM(shape, jnp.float32)

    square = several(ORB, ORB)
    half = several(HALF, HALF)
    packed = several(PACKED, HALF)
    tiles = several(*TILES)
    chunked = pltpu.SemaphoreType.DMA((2, len(CHUNKS)))
    result = pl.pallas_call(
        chain_kernel,
        out_shape=jax.ShapeDtypeStruct((ORB, ORB), jnp.bfloat16),
        in_specs=[SMEM] + [pl.BlockSpec(memory_space=pl.ANY)] * 4 + [VMEM],
        out_specs=VMEM,
        scratch_shapes=[
            square, square, square, half, half, half, square, square,
            several(3, ORB, ORB), several(3, ORB, ORB), several(2, ORB, ORB), square, square, square, square,
            several(2, 2, PACKED, HALF), several(2, 2, PACKED, HALF),
            packed, packed, packed, packed, packed, packed,
            tiles, several(TILES[0] + 16, ROWS, HALF), tiles, tiles, tiles,
            pltpu.SemaphoreType.DMA((6,)), pltpu.SemaphoreType.DMA((11,)), pltpu.SemaphoreType.DMA((11,)),
            chunked, chunked, chunked, pltpu.SemaphoreType.DMA((2, 2)),
        ],
        compiler_params=pltpu.CompilerParams(
            vmem_limit_bytes=56 * 1024 * 1024, collective_id=0, has_side_effects=True,
        ),
    )(shifts, hamilton, coupling, left_contact, right_contact, coulomb)
    return result[None, None]


def solution(mesh):
    placed = (
        P("domain", None, None),
        P("domain", None, None),
        P("energy", None, None),
        P("energy", None, None),
        P("energy"),
        P("domain", "energy", None),
    )
    return jax.shard_map(
        on_device,
        mesh=mesh,
        in_specs=placed,
        out_specs=P("energy", "domain", None, None),
        check_vma=False,
    )
```

time: 2360 us -> 161 us (0.07)
  waiting for transfers between devices: 1510 us -> 0 us
  starting transfers between devices: 548 us -> 0 us
  other arithmetic: 222 us -> 0 us
  Pallas kernels: 0 us -> 158 us
    ppermute x30 -> x0, waiting for transfers between devices: 1500 us -> none  [passed_along(): return lax.ppermute(array, axis, pairs)]
    ppermute x30 -> x0, starting transfers between devices: 509 us -> none  [passed_along(): return lax.ppermute(array, axis, pairs)]
    another operation x36 -> x0, other arithmetic: 216 us -> none  [the longest x25 137 us: spd_solve(): factor = jnp.linalg.cholesky(matrix)]
    pallas_call x0 -> x1, Pallas kernels: none -> 158 us  [on_device(): pl.pallas_call(chain_kernel, out_shape=jax.ShapeDtypeStruct((ORB, ORB), j...]
    all_to_all x1 -> x0, starting transfers between devices: 39.1 us -> none  [on_device(): lax.all_to_all(green, 'energy', split_axis=2, concat_axis=0, tiled=True)]
  transfers between devices with their start and end apart: 31 -> 0, of which waited for: 31 -> 0; matrix products, arithmetic and copies ran while one was open for 0% -> 0% of each run, Pallas kernels for 0% -> 0%
where the time goes in v1:
time: 161 us
  Pallas kernels  158 us (98%)
    pallas_call x1, Pallas kernels, on_device(): pl.pallas_call(chain_kernel, out_shape=jax.ShapeDtypeStruct((ORB, ORB), j...  158 us

profile of v1, /device:TPU:1, one launch (start us, length us, event | category | flops | bytes accessed | tf_op | source)
XLA Modules:
  0.0 160.6 jit_solution(18234592331383523886)
XLA Ops:
  0.7 158.4 %shard_map.64 = bf16[256,256]{1,0:T(8,128)(2,1)} custom-call(f32[1]{0:T(128)S(6)} %copy.8.shift, f32[1,256,256]{2,1,0:T(8,128)} %hamilton.1, f32[1,256,256]{2,1,0:T(8,128)} %coupling.1, f32[1,256,256]{2,1,0:T(8,128)} %left_contact.1, f32[1,256,256]{2,1,0:T(8,128)} %right_contact.1, f32[1,4,256]{2,1,0:T(4,128)} %coulomb.1), custom_call_target="tpu_custom_call" | custom-call | tf_op jit(solution)/shard_map/pallas_call | solution.py:420
  159.1 1.6 copy.9

commit v2 on v1

v2 whole, which is shorter than its diff:
```python
import functools

import jax
import jax.numpy as jnp
from jax import lax
from jax.experimental import pallas as pl
from jax.experimental.pallas import tpu as pltpu
from jax.sharding import PartitionSpec as P

ORB = 256
HALF = ORB // 2
ROWS = 8
HIGHEST = lax.Precision.HIGHEST
VMEM = pl.BlockSpec(memory_space=pltpu.VMEM)
SMEM = pl.BlockSpec(memory_space=pltpu.SMEM)
PACKED = ORB + ROWS


def dot(left, right, left_dim=1, right_dim=0):
    return lax.dot_general(
        left, right, (((left_dim,), (right_dim,)), ((), ())),
        precision=HIGHEST, preferred_element_type=jnp.float32,
    )


def pivot_steps(rows, first, done):
    width = rows.shape[1]
    lane = lax.broadcasted_iota(jnp.int32, rows.shape, 1)
    sublane = lax.broadcasted_iota(jnp.int32, rows.shape, 0)
    spread = [jnp.broadcast_to(rows[:, first + j:first + j + 1], (ROWS, width)) for j in range(ROWS)]
    yield
    for k in range(0, ROWS, 2):
        left, right = spread[k], spread[k + 1]
        a00, a10 = left[k:k + 1, :], left[k + 1:k + 2, :]
        a01, a11 = right[k:k + 1, :], right[k + 1:k + 2, :]
        scale = 1.0 / (a00 * a11 - a01 * a10)
        is_first, is_second = sublane == k, sublane == k + 1

        def eliminated(x0, x1, rest):
            y0 = (a11 * x0 - a01 * x1) * scale
            y1 = (a00 * x1 - a10 * x0) * scale
            return jnp.where(is_first, y0, jnp.where(is_second, y1, rest - (left * y0 + right * y1)))

        for j in range(k + 2, ROWS):
            spread[j] = eliminated(spread[j][k:k + 1, :], spread[j][k + 1:k + 2, :], spread[j])
        own0, own1 = lane == first + k, lane == first + k + 1
        x0 = jnp.where(own0[:1], 1.0, jnp.where(own1[:1], 0.0, rows[k:k + 1, :]))
        x1 = jnp.where(own1[:1], 1.0, jnp.where(own0[:1], 0.0, rows[k + 1:k + 2, :]))
        rows = eliminated(x0, x1, jnp.where(own0 | own1, 0.0, rows))
        yield
    done.append(rows)


LAZY = 8


def inverse_half(matrix):
    size = matrix.shape[0]
    count = size // ROWS
    lane = lax.broadcasted_iota(jnp.int32, (ROWS, size), 1)
    groups = [matrix[ROWS * i:ROWS * i + ROWS, :] for i in range(count)]

    def update(i, t, pivots, own):
        rows = groups[i]
        change = rows[:, ROWS * t:ROWS * t + 1] * pivots[0:1, :]
        for j in range(1, ROWS):
            change = change + rows[:, ROWS * t + j:ROWS * t + j + 1] * pivots[j:j + 1, :]
        groups[i] = jnp.where(own, 0.0, rows) - change

    done = []
    for _ in pivot_steps(groups[0], 0, done):
        pass
    groups[0] = done[0]
    for t in range(count):
        pivots = groups[t]
        own = (lane >= ROWS * t) & (lane < ROWS * t + ROWS)
        waiting = list(range(t + 2, count)) + list(range(LAZY * (t // LAZY), t))
        if t + 1 < count:
            update(t + 1, t, pivots, own)
            done = []
            share = -(-len(waiting) // (ROWS // 2 + 1))
            for _ in pivot_steps(groups[t + 1], ROWS * (t + 1), done):
                for i in waiting[:share]:
                    update(i, t, pivots, own)
                waiting = waiting[share:]
            groups[t + 1] = done[0]
        for i in waiting:
            update(i, t, pivots, own)
        if t % LAZY == LAZY - 1 and t >= LAZY:
            start = LAZY * (t // LAZY)
            before = jnp.concatenate(groups[:start], axis=0)
            run = jnp.concatenate(groups[start:start + LAZY], axis=0)
            low, high = ROWS * start, ROWS * (start + LAZY)
            columns = lax.broadcasted_iota(jnp.int32, before.shape, 1)
            kept = jnp.where((columns >= low) & (columns < high), 0.0, before)
            before = kept - dot(before[:, low:high], run)
            for i in range(start):
                groups[i] = before[ROWS * i:ROWS * i + ROWS]
    return jnp.concatenate(groups, axis=0)


def half_indices():
    row = lax.broadcasted_iota(jnp.int32, (HALF, HALF), 0)
    column = lax.broadcasted_iota(jnp.int32, (HALF, HALF), 1)
    return row, column


def pack(matrix, out):
    row, column = half_indices()
    low = matrix[HALF:, HALF:]
    out[:HALF] = matrix[:HALF, HALF:]
    out[HALF:ORB] = jnp.where(row <= column, matrix[:HALF, :HALF], low)
    diagonal = jnp.sum(jnp.where(row == column, low, 0.0), axis=0, keepdims=True)
    out[ORB:] = jnp.broadcast_to(diagonal, (ROWS, HALF))


def unpack_ends(both, diagonal):
    row, column = half_indices()
    turned = both.T
    top = jnp.where(row <= column, both, turned)
    low = jnp.where(row > column, both, turned)
    return top, jnp.where(row == column, diagonal, low)


def unpack(packed):
    corner = packed[:HALF]
    top, low = unpack_ends(packed[HALF:ORB], packed[ORB:ORB + 1])
    return jnp.concatenate(
        [jnp.concatenate([top, corner], axis=1), jnp.concatenate([corner.T, low], axis=1)], axis=0
    )


def message(source, target, send, recv, to, axis="domain"):
    return pltpu.make_async_remote_copy(
        src_ref=source, dst_ref=target, send_sem=send, recv_sem=recv,
        device_id={axis: to}, device_id_type=pl.DeviceIdType.MESH,
    )


def energy_peers():
    me = lax.axis_index("energy")
    count = lax.axis_size("energy")
    core = lax.rem(me, 2)
    return me + 1 - 2 * core, lambda k: lax.rem(me + 2 * k, count)


def energy_part(
    inverse, coulomb, out, green, landed, parity, to_twin, sums_of, from_twin, returned, final,
    own_sem, spread_sem, twin_sem,
):
    me = lax.axis_index("energy")
    chip, core = me // 2, lax.rem(me, 2)
    chips = green.shape[0]
    twin, other = energy_peers()
    first_core = core == 0

    def exchange(source, target, index):
        own = pltpu.make_async_copy(source.at[chip], target.at[chip], own_sem.at[index])
        own.start()

        def send(k, carry):
            to = other(k)
            message(
                source.at[to // 2], target.at[chip], spread_sem.at[0, index], spread_sem.at[1, index], to, "energy",
            ).start()
            return carry

        lax.fori_loop(1, chips, send, 0)
        return own, message(
            source.at[pl.ds(0, chips - 1)], target.at[pl.ds(0, chips - 1)],
            spread_sem.at[0, index], spread_sem.at[1, index], other(1), "energy",
        )

    for t in range(chips):
        rows = inverse[ROWS * t:ROWS * t + ROWS, :]
        green[t] = jnp.concatenate([rows[:, :HALF], rows[:, HALF:]], axis=0).astype(jnp.bfloat16)
    own, rest = exchange(green, landed, 0)
    pad = jnp.zeros((2, 4, ROWS, HALF), jnp.float32)
    parity[:, :4] = pad
    parity[:, 4 + chips:] = pad
    factor = jnp.concatenate([coulomb[0, :, :HALF], coulomb[0, :, HALF:]], axis=0)
    factor = factor * factor
    own.wait()
    rest.wait()
    for t in range(chips):
        both = landed[t].astype(jnp.float32)
        upper = jnp.concatenate([both[:4], both[8:12]], axis=0)
        lower = jnp.concatenate([both[4:8], both[12:]], axis=0)
        parity[core, 4 + t] = jnp.where(first_core, upper, lower)
        to_twin[t] = jnp.where(first_core, lower, upper)
    swap = message(to_twin, parity.at[core, pl.ds(4, chips)], twin_sem.at[0], twin_sem.at[1], twin, "energy")
    swap.start()
    swap.wait()

    def at(energy):
        return parity[energy % 2, 4 + energy // 2]

    blocks = 2 * chips // 8
    for kb in range(blocks):
        sums = [None] * 8
        for jb in range(blocks - kb):
            base = [at(8 * jb + a) for a in range(8)]
            ahead = [at(8 * (jb + kb) + c) for c in range(15)]
            for b in range(8):
                for a in range(8):
                    term = base[a] * ahead[a + b]
                    sums[b] = term if sums[b] is None else sums[b] + term
        for b in range(8):
            returned[8 * kb + b] = factor * sums[b]
    for kb in range(blocks):
        sums = [None] * 8
        for jb in range(kb + 1):
            base = [returned[8 * jb + a] for a in range(8)]
            behind = [at(8 * (kb - jb) + c - 7) for c in range(15)]
            for b in range(8):
                for a in range(8):
                    term = base[a] * behind[b - a + 7]
                    sums[b] = term if sums[b] is None else sums[b] + term
        for b in range(8):
            sums_of[b % 2, 4 * kb + b // 2] = sums[b]
    swap = message(sums_of.at[1 - core], from_twin, twin_sem.at[2], twin_sem.at[3], twin, "energy")
    swap.start()
    swap.wait()
    for t in range(chips):
        mine, theirs = sums_of[core, t], from_twin[t]
        upper = jnp.where(first_core, mine, theirs)
        lower = jnp.where(first_core, theirs, mine)
        both = jnp.concatenate([upper[:4], lower[:4], upper[4:], lower[4:]], axis=0)
        green[t] = both.astype(jnp.bfloat16)
    own, rest = exchange(green, final, 1)
    own.wait()
    rest.wait()
    out[...] = final[...]


ENERGY_SCRATCH = (
    ((32, 16, HALF), jnp.bfloat16), ((32, 16, HALF), jnp.bfloat16), ((2, 40, ROWS, HALF), jnp.float32),
    ((32, ROWS, HALF), jnp.float32), ((2, 32, ROWS, HALF), jnp.float32), ((32, ROWS, HALF), jnp.float32),
    ((64, ROWS, HALF), jnp.float32), ((32, 16, HALF), jnp.bfloat16),
)


def energy_scratch():
    return [pltpu.VMEM(*buffer) for buffer in ENERGY_SCRATCH] + [
        pltpu.SemaphoreType.DMA((2,)), pltpu.SemaphoreType.DMA((2, 2)), pltpu.SemaphoreType.DMA((4,)),
    ]


CHUNKS = ((128, 64), (192, 72), (0, 64), (64, 64))
ENDS, CORNER = pl.ds(HALF, PACKED - HALF), pl.ds(0, HALF)


def chain_kernel(
    shift, hamilton, coupling, left_contact, right_contact, coulomb, out,
    block, matrix, inverse, part, part_inverse, solved, lead, side,
    ups, downs, links, toward, away, longer, across,
    to_ring, from_ring, to_pair, from_pair, to_middle, middle, settled, distant, opposite,
    load_sem, send_sem, recv_sem, pair_sem, near_sem, far_sem, middle_sem,
    green, landed, parity, to_twin, sums_of, from_twin, returned, final, own_sem, spread_sem, twin_sem,
):
    place = lax.axis_index("domain")
    count = lax.axis_size("domain")
    chips = green.shape[0]
    twin, other = energy_peers()
    quarter = place // 4
    inner = (place >= 4) & (place < 12)
    odd = lax.rem(quarter, 2)
    even = odd == 0
    pair, near, far = place + 4 - 8 * odd, place + 12 - 8 * quarter, lax.rem(place + 8, count)
    loads = [
        pltpu.make_async_copy(source.at[0], target, load_sem.at[i])
        for i, (source, target) in enumerate(
            ((hamilton, block), (coupling, ups.at[0]), (left_contact, lead), (right_contact, side))
        )
    ]
    for load in loads:
        load.start()

    def neighbour(by):
        return lax.rem(place + by + count, count)

    peers = [neighbour(1), neighbour(-1), neighbour(2), neighbour(-2), pair, near, far]
    barrier = pltpu.get_barrier_semaphore()
    for peer in peers:
        pl.semaphore_signal(barrier, inc=1, device_id={"domain": peer}, device_id_type=pl.DeviceIdType.MESH)

    def greet(k, carry):
        pl.semaphore_signal(barrier, inc=1, device_id={"energy": other(k)}, device_id_type=pl.DeviceIdType.MESH)
        return carry

    lax.fori_loop(1, chips, greet, 0)
    pl.semaphore_signal(barrier, inc=1, device_id={"energy": twin}, device_id_type=pl.DeviceIdType.MESH)
    first_link = message(coupling.at[0], downs.at[0], send_sem.at[0], recv_sem.at[0], neighbour(-1))

    def ring_messages(turn):
        stride = turn + 1
        left, right = neighbour(-stride), neighbour(stride)
        base = 1 + 6 * turn
        return [
            message(
                to_ring.at[turn, side_id, rows], from_ring.at[turn, side_id, rows],
                send_sem.at[base + i], recv_sem.at[base + i], to,
            )
            for i, (side_id, rows, to) in enumerate(
                ((0, ENDS, left), (1, ENDS, right), (0, CORNER, left), (1, CORNER, right))
            )
        ] + [
            message(links.at[turn], downs.at[turn + 1], send_sem.at[base + 4], recv_sem.at[base + 4], left),
            message(links.at[turn], ups.at[turn + 1], send_sem.at[base + 5], recv_sem.at[base + 5], right),
        ]

    def chunk_messages(source, target, send, recv, to):
        return [
            message(source.at[pl.ds(*rows)], target.at[pl.ds(*rows)], send.at[i], recv.at[i], to)
            for i, rows in enumerate(CHUNKS)
        ]

    pair_messages = chunk_messages(to_pair, from_pair, pair_sem.at[0], pair_sem.at[1], pair)
    near_messages = chunk_messages(settled, opposite, near_sem.at[0], near_sem.at[1], near)
    far_messages = chunk_messages(distant, opposite, far_sem.at[0], near_sem.at[1], far)
    middle_messages = chunk_messages(to_middle, middle, middle_sem.at[0], middle_sem.at[1], near)
    link_message = message(longer, across, send_sem.at[13], recv_sem.at[13], pair)

    def before_first():
        for load in loads:
            load.wait()
        row = lax.broadcasted_iota(jnp.int32, (ORB, ORB), 0)
        column = lax.broadcasted_iota(jnp.int32, (ORB, ORB), 1)
        block[...] += jnp.where(row == column, shift[0], 0.0)

        @pl.when(place == 0)
        def _():
            link = ups[0]
            block[...] += dot(link, dot(lead[...], link), 0, 0)
            ups[0] = jnp.zeros((ORB, ORB), jnp.float32)

        @pl.when(place == count - 1)
        def _():
            block[...] += side[...]

        matrix[...] = block[...]

    def before_ring(turn):
        messages = ring_messages(turn)
        messages[0].wait_recv()
        messages[1].wait_recv()

        @pl.when(turn == 0)
        def _():
            messages[2].wait_recv()
            messages[3].wait_recv()
            left_inverse = unpack(from_ring[0, 1])
            block[...] -= dot(ups[0], dot(left_inverse, ups[0]), 0, 0)
            block[...] -= unpack(from_ring[0, 0])
            matrix[...] = block[...]

        @pl.when(turn == 1)
        def _():
            ends = from_ring[1, 0, HALF:, :] + from_ring[1, 1, HALF:, :]
            top, low = unpack_ends(ends[:HALF], ends[HALF:HALF + 1])
            block[:HALF, :HALF] -= top
            block[HALF:, HALF:] -= low
            matrix[:HALF, :HALF] = block[:HALF, :HALF]
            matrix[HALF:, HALF:] = block[HALF:, HALF:]

    def before_ring_corner():
        for received in ring_messages(1)[2:4]:
            received.wait_recv()
        corner = block[:HALF, HALF:] - from_ring[1, 0, :HALF, :] - from_ring[1, 1, :HALF, :]
        block[:HALF, HALF:] = corner
        block[HALF:, :HALF] = corner.T
        matrix[:HALF, HALF:] = corner

    def before_middle():
        @pl.when(inner)
        def _():
            pack(block[...], settled)
            for i, rows in enumerate(CHUNKS):
                pair_messages[i].wait_recv()
                settled[pl.ds(*rows)] -= from_pair[pl.ds(*rows)]
                near_messages[i].start()
                middle_messages[i].wait_recv()
                distant[pl.ds(*rows)] = settled[pl.ds(*rows)] - middle[pl.ds(*rows)]
                far_messages[i].start()
            block[...] = unpack(settled[...])
            for received in near_messages[:2]:
                received.wait_recv()

        @pl.when(jnp.logical_not(inner))
        def _():
            for received in pair_messages:
                received.wait_recv()
            block[...] -= unpack(from_pair[...])
            for received in far_messages[:2]:
                received.wait_recv()

        ends = opposite[HALF:, :]
        top, low = unpack_ends(ends[:HALF], ends[HALF:HALF + 1])
        matrix[:HALF, :HALF] = top
        matrix[HALF:, HALF:] = low

    def before_middle_corner():
        for received in near_messages[2:]:
            received.wait_recv()
        matrix[:HALF, HALF:] = opposite[:HALF, :]

    def before_last():
        @pl.when(inner)
        def _():
            across[...] = away[...].T

        @pl.when(jnp.logical_not(inner))
        def _():
            link_message.wait_recv()

        link = across[...]
        block[...] -= dot(link, dot(inverse[...], link), 0, 0)
        matrix[...] = block[...]

    def after_ring(turn):
        messages = ring_messages(turn)

        @pl.when(turn == 0)
        def _():
            pack(inverse[...], to_ring.at[turn, 1])
            messages[1].start()
            messages[3].start()

        @pl.when(turn == 1)
        def _():
            for received in ring_messages(0)[4:]:
                received.wait_recv()

        pack(dot(ups[turn], dot(inverse[...], ups[turn], 1, 1)), to_ring.at[turn, 0])
        messages[0].start()
        messages[2].start()

        @pl.when(turn == 0)
        def _():
            first_link.wait_recv()

            @pl.when(place == count - 1)
            def _():
                downs[0] = jnp.zeros((ORB, ORB), jnp.float32)

        matrix[...] = dot(inverse[...], downs[turn])

        @pl.when(turn == 1)
        def _():
            pack(dot(downs[turn], matrix[...], 0, 0), to_ring.at[turn, 1])
            messages[1].start()
            messages[3].start()

        links[turn] = -dot(ups[turn], matrix[...])
        messages[4].start()
        messages[5].start()

    def after_pair():
        for received in ring_messages(1)[4:]:
            received.wait_recv()
        turned = ups[2].T
        toward[...] = jnp.where(even, downs[2], turned)
        pack(dot(toward[...], dot(inverse[...], toward[...]), 0, 0), to_pair)
        for sent in pair_messages:
            sent.start()
        away[...] = jnp.where(even, turned, downs[2])

        @pl.when(inner)
        def _():
            matrix[...] = dot(inverse[...], away[...])
            pack(dot(away[...], matrix[...], 0, 0), to_middle)
            for sent in middle_messages:
                sent.start()
            longer[...] = -dot(matrix[...], toward[...], 0, 0)
            link_message.start()

    def turn_half(step, carry):
        turn, half = step // 2, lax.rem(step, 2)

        @pl.when(step == 1)
        def _():
            pl.semaphore_wait(barrier, len(peers) + chips)
            first_link.start()

        @pl.when(half == 0)
        def _():
            pl.when(turn == 0)(before_first)
            pl.when((turn == 1) | (turn == 2))(lambda: before_ring(turn - 1))
            pl.when(turn == 3)(before_middle)
            pl.when(turn == 4)(before_last)
            part[...] = matrix[:HALF, :HALF]

        @pl.when(half == 1)
        def _():
            pl.when(turn == 2)(before_ring_corner)
            pl.when(turn == 3)(before_middle_corner)
            top = part_inverse[...]
            corner = matrix[:HALF, HALF:]
            inverse[:HALF, :HALF] = top
            solved[...] = dot(top, corner)
            part[...] = matrix[HALF:, HALF:] - dot(corner, solved[...], 0, 0)

        part_inverse[...] = inverse_half(part[...])

        @pl.when(half == 1)
        def _():
            low = part_inverse[...]
            corner = dot(solved[...], low)
            inverse[:HALF, :HALF] += dot(corner, solved[...], 1, 1)
            inverse[:HALF, HALF:] = -corner
            inverse[HALF:, :HALF] = -corner.T
            inverse[HALF:, HALF:] = low
            pl.when(turn <= 1)(lambda: after_ring(turn))
            pl.when(turn == 2)(after_pair)

        return carry

    lax.fori_loop(0, 10, turn_half, 0)
    energy_part(
        inverse, coulomb, out, green, landed, parity, to_twin, sums_of, from_twin, returned, final,
        own_sem, spread_sem, twin_sem,
    )
    first_link.wait_send()
    for turn in range(2):
        for sent in ring_messages(turn):
            sent.wait_send()
    for sent in pair_messages:
        sent.wait_send()

    @pl.when(inner)
    def _():
        for sent in (link_message, *middle_messages, *near_messages, *far_messages):
            sent.wait_send()


def on_device(hamilton, coupling, left_contact, right_contact, shifts, coulomb):
    def several(*shape):
        return pltpu.VMEM(shape, jnp.float32)

    square = several(ORB, ORB)
    half = several(HALF, HALF)
    packed = several(PACKED, HALF)
    chunked = pltpu.SemaphoreType.DMA((2, len(CHUNKS)))
    result = pl.pallas_call(
        chain_kernel,
        out_shape=jax.ShapeDtypeStruct((ORB // ROWS, 2 * ROWS, HALF), jnp.bfloat16),
        in_specs=[SMEM] + [pl.BlockSpec(memory_space=pl.ANY)] * 4 + [VMEM],
        out_specs=VMEM,
        scratch_shapes=[
            square, square, square, half, half, half, square, square,
            several(3, ORB, ORB), several(3, ORB, ORB), several(2, ORB, ORB), square, square, square, square,
            several(2, 2, PACKED, HALF), several(2, 2, PACKED, HALF),
            packed, packed, packed, packed, packed, packed, packed,
            pltpu.SemaphoreType.DMA((4,)), pltpu.SemaphoreType.DMA((14,)), pltpu.SemaphoreType.DMA((14,)),
            chunked, chunked, chunked, chunked, *energy_scratch(),
        ],
        compiler_params=pltpu.CompilerParams(
            vmem_limit_bytes=56 * 1024 * 1024, collective_id=0, has_side_effects=True,
        ),
    )(shifts, hamilton, coupling, left_contact, right_contact, coulomb)
    result = result.reshape(ORB // ROWS, 2, ROWS, HALF).transpose(0, 2, 1, 3)
    return result.reshape(1, 1, ORB, ORB)


def solution(mesh):
    placed = (
        P("domain", None, None),
        P("domain", None, None),
        P("energy", None, None),
        P("energy", None, None),
        P("energy"),
        P("domain", "energy", None),
    )
    return jax.shard_map(
        on_device,
        mesh=mesh,
        in_specs=placed,
        out_specs=P("energy", "domain", None, None),
        check_vma=False,
    )
```

time: 161 us -> 146 us (0.907)
  the two profiles are of different devices: /device:TPU:1 before, /device:TPU:128 now
where the time goes in v2:
time: 146 us
  Pallas kernels  144 us (99%)
  local copies, waits for them, and re-layouts  1.57 us (1%)
    pallas_call x1, Pallas kernels, on_device(): pl.pallas_call(chain_kernel, out_shape=jax.ShapeDtypeStruct((ORB // ROWS,...  144 us

profile of v2, /device:TPU:128, one launch (start us, length us, event | category | flops | bytes accessed | tf_op | source)
XLA Modules:
  0.0 146.3 jit_solution(10235402801291343000)
XLA Ops:
  0.7 144.1 %shard_map.64 = bf16[32,16,128]{2,1,0:T(8,128)(2,1)} custom-call(f32[1]{0:T(128)S(6)} %copy.8.shift, f32[1,256,256]{2,1,0:T(8,128)} %hamilton.1, f32[1,256,256]{2,1,0:T(8,128)} %coupling.1, f32[1,256,256]{2,1,0:T(8,128)} %left_contact.1, f32[1,256,256]{2,1,0:T(8,128)} %right_contact.1, f32[1,4,256]{2,1,0:T(4,128)} %coulomb.1), custom_call_target="tpu_custom_call" | custom-call | tf_op jit(solution)/shard_map/pallas_call | solution.py:544
  144.7 1.6 %copy.9 = bf16[1,1,256,256]{3,2,1,0:T(8,128)(2,1)} copy(bf16[1,1,256,256]{3,2,1,0:T(8,128)(2,1)} %bitcast.5) | data formatting | bytes 262144

commit v3 on v2

--- a/solution.py
+++ b/solution.py
@@ -159,7 +159,7 @@
         own.start()
 
         def send(k, carry):
-            to = other(k)
+            to = other(lax.rem(k + chips // 2 - 2, chips - 1) + 1)
             message(
                 source.at[to // 2], target.at[chip], spread_sem.at[0, index], spread_sem.at[1, index], to, "energy",
             ).start()
@@ -460,17 +460,21 @@
             received.wait_recv()
         turned = ups[2].T
         toward[...] = jnp.where(even, downs[2], turned)
-        pack(dot(toward[...], dot(inverse[...], toward[...]), 0, 0), to_pair)
-        for sent in pair_messages:
-            sent.start()
-        away[...] = jnp.where(even, turned, downs[2])
 
         @pl.when(inner)
         def _():
+            away[...] = jnp.where(even, turned, downs[2])
             matrix[...] = dot(inverse[...], away[...])
             pack(dot(away[...], matrix[...], 0, 0), to_middle)
             for sent in middle_messages:
                 sent.start()
+
+        pack(dot(toward[...], dot(inverse[...], toward[...]), 0, 0), to_pair)
+        for sent in pair_messages:
+            sent.start()
+
+        @pl.when(inner)
+        def _():
             longer[...] = -dot(matrix[...], toward[...], 0, 0)
             link_message.start()
 

time: 146 us -> 147 us (level)
  no operation moved by 1% of the time
where the time goes in v3:
time: 147 us
  Pallas kernels  145 us (99%)
  local copies, waits for them, and re-layouts  1.57 us (1%)
    pallas_call x1, Pallas kernels, on_device(): pl.pallas_call(chain_kernel, out_shape=jax.ShapeDtypeStruct((ORB // ROWS,...  145 us

profile of v3, /device:TPU:128, one launch (start us, length us, event | category | flops | bytes accessed | tf_op | source)
XLA Modules:
  0.0 147.0 jit_solution(5262365607970800272)
XLA Ops:
  0.7 144.8 %shard_map.64 = bf16[32,16,128]{2,1,0:T(8,128)(2,1)} custom-call(f32[1]{0:T(128)S(6)} %copy.8.shift, f32[1,256,256]{2,1,0:T(8,128)} %hamilton.1, f32[1,256,256]{2,1,0:T(8,128)} %coupling.1, f32[1,256,256]{2,1,0:T(8,128)} %left_contact.1, f32[1,256,256]{2,1,0:T(8,128)} %right_contact.1, f32[1,4,256]{2,1,0:T(4,128)} %coulomb.1), custom_call_target="tpu_custom_call" | custom-call | tf_op jit(solution)/shard_map/pallas_call | solution.py:548
  145.5 1.6 %copy.9 = bf16[1,1,256,256]{3,2,1,0:T(8,128)(2,1)} copy(bf16[1,1,256,256]{3,2,1,0:T(8,128)(2,1)} %bitcast.5) | data formatting | bytes 262144
